TPU v7x, 256 devices: a whole 4x4x8 slice. The times are simulated.
256 devices in a mesh: expert: 64 (over z, x, core), mp: 4 (over y).
Axes of the slice: x: 4, y: 4, z: 8, core: 2. Of those that a mesh axis runs over, the one named last changes fastest.
Arguments:
- tokens: bfloat16 [32768, 4096], P('expert', 'mp'), may hold values from -400 to 400
- norm_gain: bfloat16 [4096], P('mp'), may hold values from 0.099609375 to 1.8984375
- router: bfloat16 [4096, 16], replicated, may hold values from -0.09375 to 0.09375
- w_gate: bfloat16 [64, 4096, 1536], P('expert', None, 'mp'), may hold values from -0.09375 to 0.09375
- w_up: bfloat16 [64, 4096, 1536], P('expert', None, 'mp'), may hold values from -0.09375 to 0.09375
- w_down: bfloat16 [64, 1536, 4096], P('expert', 'mp'), may hold values from -0.078125 to 0.078125
- picked: int32 [16, 512], replicated, may hold values from 0 to 32767, as said below
Outputs:
- moe_out: bfloat16 [32768, 4096], P('expert', 'mp')
Inputs may be any that keep to these rules, and one draw needn't show every extreme that they name: `picked`: each row names 512 distinct tokens; at most 16 of them lie among the 512 tokens of one index of expert, and for every expert exactly 16 lie among some one device's tokens.
All inputs are finite; a program needn't handle non-finite values.
Results may differ from a plain program's by a relative error of at most 0.0071.
Values may be sent and summed in bfloat16 or wider, within the bound.
A program may use at most 128 MiB of HBM per device.

v0:
```python
import jax
import jax.numpy as jnp
from jax import lax
from jax.sharding import PartitionSpec as P

SLICES = 4
CAP = 16


epsilon = 1e-06


def per_device(tokens, norm_gain, router, w_gate, w_up, w_down, picked):
    tok_dev, quarter = tokens.shape
    experts_n, capacity = picked.shape
    owners = lax.axis_size("expert")
    my_index = lax.axis_index("expert")
    mp_index = lax.axis_index("mp")
    mp_count = lax.axis_size("mp")
    slot_cap = CAP
    model_width = quarter * mp_count
    tok_float = tokens.astype(jnp.float32)
    norm_sum = lax.psum(jnp.sum(tok_float * tok_float, axis=-1), "mp")
    scale_inv = lax.rsqrt(norm_sum / model_width + epsilon)
    normed = (tok_float * scale_inv[:, None] * norm_gain.astype(jnp.float32)[None, :]).astype(
        jnp.bfloat16
    )
    owner_of = picked // tok_dev
    local_idx = picked % tok_dev
    onehot = (owner_of[:, :, None] == jnp.arange(owners, dtype=jnp.int32)[None, None, :]).astype(
        jnp.int32
    )
    running = jnp.cumsum(onehot, axis=1)
    slot_rank = jnp.take_along_axis(running, owner_of[:, :, None], axis=2)[:, :, 0] - 1
    expert_ids = jnp.broadcast_to(
        jnp.arange(experts_n, dtype=jnp.int32)[:, None], (experts_n, capacity)
    )
    is_mine = owner_of == my_index
    column_at = jnp.where(is_mine, slot_rank, slot_cap)
    value_at = jnp.where(is_mine, local_idx, tok_dev)
    slot_tok = (
        jnp.full((experts_n, slot_cap + 1), tok_dev, jnp.int32)
        .at[expert_ids, column_at]
        .set(value_at)[:, :slot_cap]
    )
    normed_pad = jnp.concatenate([normed, jnp.zeros((1, quarter), jnp.bfloat16)], axis=0)
    outgoing = jnp.repeat(jnp.take(normed_pad, slot_tok, axis=0), SLICES, axis=0)
    my_expert = my_index // SLICES
    my_owner = lax.dynamic_index_in_dim(owner_of, my_expert, 0, keepdims=False)
    my_rank = lax.dynamic_index_in_dim(slot_rank, my_expert, 0, keepdims=False)
    flat_slot = my_owner * slot_cap + my_rank
    router_rows = lax.dynamic_slice_in_dim(router, mp_index * quarter, quarter, 0)
    partial_logits = jnp.dot(normed, router_rows, preferred_element_type=jnp.float32)
    logits = lax.psum(partial_logits, "mp")
    gate_local = jax.nn.sigmoid(logits).astype(jnp.bfloat16)
    gate_pad = jnp.concatenate([gate_local, jnp.zeros((1, experts_n), jnp.bfloat16)], axis=0)
    gate_slots = gate_pad[slot_tok, jnp.arange(experts_n, dtype=jnp.int32)[:, None]]
    gate_out = jnp.repeat(gate_slots, SLICES, axis=0)
    incoming, gate_in = (
        lax.all_to_all(outgoing, "expert", split_axis=0, concat_axis=0, tiled=True),
        lax.all_to_all(gate_out, "expert", split_axis=0, concat_axis=0, tiled=True),
    )
    gate_vals = jnp.take(gate_in.reshape(-1), flat_slot, axis=0)
    picked_rows = jnp.take(incoming.reshape(-1, quarter), flat_slot, axis=0)
    weight_gate = w_gate[0]
    weight_up = w_up[0]
    weight_down = w_down[0]
    shard_piece = lax.all_gather(picked_rows, "mp", axis=1, tiled=True)
    hidden = (
        jax.nn.gelu(
            jnp.dot(shard_piece, weight_gate, preferred_element_type=jnp.float32), approximate=True
        )
        * jnp.dot(shard_piece, weight_up, preferred_element_type=jnp.float32)
    ).astype(jnp.bfloat16)
    gate_float = gate_vals.astype(jnp.float32)[:, None]
    slot_to_row = (
        jnp.full((owners * slot_cap,), capacity, jnp.int32)
        .at[flat_slot]
        .set(jnp.arange(capacity, dtype=jnp.int32))
    )
    tok_of = jnp.repeat(slot_tok, SLICES, axis=0).reshape(-1)
    product = jnp.dot(hidden, weight_down, preferred_element_type=jnp.float32)
    summed = lax.psum_scatter(
        jnp.transpose(product.reshape(capacity, lax.axis_size("mp") * 1, quarter), (1, 0, 2)),
        "mp",
        scatter_dimension=0,
        tiled=True,
    )[0]
    incoming_fn = lambda returning: lax.all_to_all(
        returning, "expert", split_axis=0, concat_axis=0, tiled=True
    )
    gated = summed * gate_float
    gated_pad = jnp.concatenate([gated, jnp.zeros((1, quarter), jnp.float32)], axis=0)
    send_returning = jnp.take(gated_pad, slot_to_row, axis=0).reshape(owners, slot_cap, quarter)
    arrived = incoming_fn(send_returning)
    summed_tokens = (
        jnp.zeros((tok_dev + 1, quarter), jnp.float32).at[tok_of].add(arrived.reshape(-1, quarter))
    )
    result_rows = summed_tokens[:tok_dev]
    return result_rows.astype(jnp.bfloat16)


def solution(mesh):
    return jax.shard_map(
        per_device,
        mesh=mesh,
        in_specs=(
            P("expert", "mp"),
            P("mp"),
            P(),
            P("expert", None, "mp"),
            P("expert", None, "mp"),
            P("expert", "mp", None),
            P(),
        ),
        out_specs=P("expert", "mp"),
        check_vma=False,
    )
```

profile of v0, /device:TPU:1, one launch (start us, length us, event | category | flops | bytes accessed | tf_op | source)
XLA Modules:
  0.0 651.1 jit_solution(18155708924784575065)
XLA Ops:
  6.5 0.9 fusion.31
  7.5 1.6 fusion.7
  9.1 36.4 %reduce-window.6 = s32[16,64,4,128]{3,1,2,0:T(8,128)} reduce-window(s32[16,64,4,128]{3,1,2,0:T(8,128)} %fusion.7, s32[]{:T(128)} %constant.104.clone.1), window={size=1x1x1x128 pad=0_0x0_0x0_0x127_0}, to_apply=%region_0.0 | reduce-window | flops 66584576 | bytes 4194308 | tf_op jit(solution)/shard_map/reduce-window
  45.5 3.5 slice.30
  49.0 2.3 copy.17
  51.3 0.1 fusion.39
  51.4 2.9 bitcast_bitcast_fusion
  54.4 152.9 %gather_fusion.5 = s32[8192]{0:T(1024)S(1)} fusion(s32[16,512,64]{1,2,0:T(8,128)} %bitcast_bitcast_fusion, s32[8192]{0:T(1024)S(1)} %bitcast.73), kind=kCustom, calls=%fused_computation.5 | custom fusion | bytes 163840 | tf_op jit(solution)/shard_map/jit(take_along_axis)/gather | solution.py:34
  207.5 0.1 and_reduce_fusion
  207.7 30.4 %scatter_custom_fusion.2 = s32[272]{0:T(512)S(1)} fusion(s32[8192]{0:T(1024)S(1)} %bitcast.80, s32[8192]{0:T(1024)S(1)} %bitcast.81, s32[]{:T(128)} %constant.96.clone.1), kind=kCustom, calls=%fused_computation.92 | custom fusion | bytes 1092
  238.2 1.5 fusion.4
  239.7 9.6 %psum.14 = f32[512]{0:T(512)S(1)} all-reduce(f32[512]{0:T(512)S(1)} %fusion.4), channel_id=1, replica_groups=mesh['expert'=64,'mp'=4] {'mp'}, use_global_device_ids=true, to_apply=%region_5.6 | all-reduce | flops 512 | bytes 4096 | tf_op jit(solution)/shard_map/psum | solution.py:23
  249.3 2.5 fusion.6
  251.8 1.6 fusion.41
  253.4 10.9 %psum.15 = f32[512,16]{0,1:T(8,128)S(1)} all-reduce(f32[512,16]{0,1:T(8,128)S(1)} %fusion.41), channel_id=1, replica_groups=mesh['expert'=64,'mp'=4] {'mp'}, use_global_device_ids=true, to_apply=%region_7.8 | all-reduce | flops 8192 | bytes 65536 | tf_op jit(solution)/shard_map/psum | solution.py:54
  264.5 2.5 gather_fusion.2
  267.0 0.1 reshape.199
  267.1 0.6 copy.21
  267.8 17.7 %all-to-all-start.1 = ((bf16[64,1,16]{2,1,0:T(2,128)(2,1)}), bf16[64,1,16]{2,1,0:T(2,128)(2,1)S(1)}, u32[]{:S(2)}, u32[]{:S(2)}) async-start(bf16[64,1,16]{2,1,0:T(2,128)(2,1)} %copy.21), calls=%async_computation.2 | async-start | bytes 65536 | tf_op jit(solution)/shard_map/all_to_all | solution.py:61
  285.4 2.3 concatenate.16
  287.8 3.7 gather_fusion
  291.5 2.0 broadcast_select_fusion.2
  293.5 1.3 all-to-all-done.1
  294.8 2.6 broadcast_in_dim.107
  297.4 9.2 %all-to-all-start = ((bf16[64,16,1024]{2,1,0:T(8,128)(2,1)}), bf16[64,16,1024]{2,1,0:T(8,128)(2,1)}, u32[]{:S(2)}, u32[]{:S(2)}) async-start(bf16[64,16,1024]{2,1,0:T(8,128)(2,1)} %bitcast.76), calls=%async_computation | async-start | bytes 4194304 | tf_op jit(solution)/shard_map/all_to_all | solution.py:60
  306.7 0.1 reduce.2
  306.8 0.1 reshape.174
  306.9 3.5 gather_fusion.3
  310.4 45.8 %all-to-all-done = bf16[64,16,1024]{2,1,0:T(8,128)(2,1)} async-done(((bf16[64,16,1024]{2,1,0:T(8,128)(2,1)}), bf16[64,16,1024]{2,1,0:T(8,128)(2,1)}, u32[]{:S(2)}, u32[]{:S(2)}) %all-to-all-start) | async-done | bytes 2097184 | tf_op jit(solution)/shard_map/all_to_all | solution.py:60
  356.2 5.3 gather_fusion.1
  361.5 2.4 broadcast_select_fusion.1
  363.9 0.2 reduce-scatter.2.cloned.1.call-start
  364.1 4.7 copy.22
  368.8 42.6 %all-gather.2.cloned.1.call-done = bf16[512,4096]{1,0:T(8,128)(2,1)} async-done(((bf16[512,1024]{1,0:T(8,128)(2,1)}), bf16[512,4096]{1,0:T(8,128)(2,1)}) %all-gather.2.cloned.1.call-update) | async-done | bytes 4194320 | tf_op jit(solution)/shard_map/all_gather | solution.py:68
  411.4 6.5 fusion.27
  417.9 11.1 %convolution_bitcast_fusion = f32[4,512,1024]{2,1,0:T(8,128)} fusion(bf16[4,1024,384]{2,1,0:T(8,128)(2,1)} %bitcast.74, f32[512,384]{1,0:T(8,128)} %fusion.27, bf16[512,4096]{1,0:T(8,128)(2,1)} %all-gather.2.cloned.1.call-done, bf16[1,4096,384]{2,1,0:T(8,128)(2,1)S(1)} %copy-done), kind=kOutput, calls=%fused_computation.9 | convolution fusion | flops 3221618688 | bytes 19660800 | tf_op jit(solution)/shard_map/dot_general | solution.py:82
  429.0 2.4 scatter_custom_fusion
  431.5 0.1 broadcast_in_dim.101
  431.6 81.1 %reduce-scatter.2.cloned.1.call-done = f32[1,512,1024]{2,1,0:T(8,128)} async-done(((f32[4,512,1024]{2,1,0:T(8,128)}), f32[1,512,1024]{2,1,0:T(8,128)}) %reduce-scatter.2.cloned.1.call-update) | async-done | bytes 2097168 | tf_op jit(solution)/shard_map/reduce_scatter | solution.py:83
  512.7 1.8 bitcast_multiply_fusion
  514.5 0.1 concatenate.19
  514.6 5.4 gather_fusion.4
  520.1 4.5 broadcast_select_fusion
  524.6 10.8 %all-to-all-start.2 = ((f32[64,16,1024]{2,1,0:T(8,128)}), f32[64,16,1024]{2,1,0:T(8,128)}, u32[]{:S(2)}, u32[]{:S(2)}) async-start(f32[64,16,1024]{2,1,0:T(8,128)} %broadcast_select_fusion), calls=%async_computation.3 | async-start | bytes 8388608 | tf_op jit(solution)/shard_map/all_to_all | solution.py:89
  535.4 0.1 reshape_reshape.3
  535.5 94.3 %all-to-all-done.2 = f32[64,16,1024]{2,1,0:T(8,128)} async-done(((f32[64,16,1024]{2,1,0:T(8,128)}), f32[64,16,1024]{2,1,0:T(8,128)}, u32[]{:S(2)}, u32[]{:S(2)}) %all-to-all-start.2) | async-done | bytes 4194336 | tf_op jit(solution)/shard_map/all_to_all | solution.py:89
  629.8 11.7 %scatter_custom_fusion.1 = f32[513,1024]{1,0:T(8,128)} fusion(s32[1024]{0:T(1024)S(1)} %bitcast.85, f32[1024,1024]{1,0:T(8,128)} %bitcast.23, f32[]{:T(128)} %constant.95.clone.1), kind=kCustom, calls=%fused_computation.30 | custom fusion | flops 1048576 | bytes 2101760 | tf_op jit(solution)/shard_map/scatter-add | solution.py:97
  641.5 2.7 slice.62
  (49 shorter events, 0.7 us)
Async XLA Ops:
  6.5 411.3 %copy-start = (bf16[1,4096,384]{2,1,0:T(8,128)(2,1)S(1)}, bf16[1,4096,384]{2,1,0:T(8,128)(2,1)}, u32[]{:S(2)}) copy-start(bf16[1,4096,384]{2,1,0:T(8,128)(2,1)} %param.11) | copy-start | bytes 9437188
  54.4 153.0 %copy-start.4 = (s32[2]{0:T(128)S(1)}, s32[2]{0:T(128)}, u32[]{:S(2)}) copy-start(s32[2]{0:T(128)} %constant.185) | copy-start | bytes 28
  54.4 153.1 %copy-start.3 = (s32[2]{0:T(128)S(1)}, s32[2]{0:T(128)}, u32[]{:S(2)}) copy-start(s32[2]{0:T(128)} %constant.182) | copy-start | bytes 28
  54.4 183.8 %copy-start.2 = (bf16[1024]{0:T(1024)(128)(2,1)S(1)}, bf16[1024]{0:T(1024)(128)(2,1)}, u32[]{:S(2)}) copy-start(bf16[1024]{0:T(1024)(128)(2,1)} %param.8) | copy-start | bytes 6148
  267.8 27.0 %all-to-all-start.1 = ((bf16[64,1,16]{2,1,0:T(2,128)(2,1)}), bf16[64,1,16]{2,1,0:T(2,128)(2,1)S(1)}, u32[]{:S(2)}, u32[]{:S(2)}) async-start(bf16[64,1,16]{2,1,0:T(2,128)(2,1)} %copy.21), calls=%async_computation.2 | async-start | bytes 65536 | tf_op jit(solution)/shard_map/all_to_all | solution.py:61
  297.4 58.8 %all-to-all-start = ((bf16[64,16,1024]{2,1,0:T(8,128)(2,1)}), bf16[64,16,1024]{2,1,0:T(8,128)(2,1)}, u32[]{:S(2)}, u32[]{:S(2)}) async-start(bf16[64,16,1024]{2,1,0:T(8,128)(2,1)} %bitcast.76), calls=%async_computation | async-start | bytes 4194304 | tf_op jit(solution)/shard_map/all_to_all | solution.py:60
  306.6 104.8 %all-gather.2.cloned.1.call-start = ((), (), s32[]{:S(2)}) async-start(), calls=%async_computation.4 | async-start | bytes 5242880 | tf_op jit(solution)/shard_map/all_gather | solution.py:68
  363.9 148.8 %reduce-scatter.2.cloned.1.call-start = ((), (), s32[]{:S(2)}) async-start(), calls=%async_computation.5 | async-start | bytes 10485760 | tf_op jit(solution)/shard_map/reduce_scatter | solution.py:83
  524.6 105.2 %all-to-all-start.2 = ((f32[64,16,1024]{2,1,0:T(8,128)}), f32[64,16,1024]{2,1,0:T(8,128)}, u32[]{:S(2)}, u32[]{:S(2)}) async-start(f32[64,16,1024]{2,1,0:T(8,128)} %broadcast_select_fusion), calls=%async_computation.3 | async-start | bytes 8388608 | tf_op jit(solution)/shard_map/all_to_all | solution.py:89
  535.4 108.9 %copy-start.1 = (bf16[1,4096,384]{2,1,0:T(8,128)(2,1)S(1)}, bf16[1,4096,384]{2,1,0:T(8,128)(2,1)}, u32[]{:S(2)}) copy-start(bf16[1,4096,384]{2,1,0:T(8,128)(2,1)} %param.11) | copy-start | bytes 9437188
Sparse Core Ops, SparseCore 0:
  364.0 47.3 all-gather.1
  429.1 83.5 reduce-scatter.1
where the time goes:
time: 662 us; the launch traced here: 651 us
  waiting for transfers between devices  265 us (40%)
  local copies, waits for them, and re-layouts  226 us (34%)
  other arithmetic  68.7 us (10%)
  starting transfers between devices  37.9 us (6%)
  blocking collectives  20.5 us (3%)
  matrix products  19.2 us (3%)
  between operations  13.8 us (2%)
    gather x2, local copies, waits for them, and re-layouts, per_device(): jnp.take_along_axis(running, owner_of[:, :, None], axis=2)[:, :, 0] - 1  153 us
    all_to_all x1, waiting for transfers between devices, per_device(): lax.all_to_all(returning, 'expert', split_axis=0, concat_axis=0, tiled=True)  94.3 us
    reduce_scatter x1, waiting for transfers between devices, per_device(): lax.psum_scatter(jnp.transpose(product.reshape(capacity, lax.axis_size('m...  81.1 us
    all_to_all x1, waiting for transfers between devices, per_device(): lax.all_to_all(outgoing, 'expert', split_axis=0, concat_axis=0, tiled=True)  45.8 us
    all_gather x1, waiting for transfers between devices, per_device(): shard_piece = lax.all_gather(picked_rows, 'mp', axis=1, tiled=True)  42.6 us
    another operation x3, other arithmetic  39.4 us
    unnamed x16, local copies, waits for them, and re-layouts  30.5 us
    all_to_all x1, starting transfers between devices, per_device(): lax.all_to_all(gate_out, 'expert', split_axis=0, concat_axis=0, tiled=True)  17.7 us
  transfers between devices with their start and end apart: 5, of which 5 were waited for; matrix products, arithmetic and copies ran while one was open for 3% of the time, Pallas kernels for 0%

commit v1 on v0

v1 whole, which is shorter than its diff:
```python
import functools

import jax
import jax.numpy as jnp
from jax import lax
from jax.experimental import pallas as pl
from jax.experimental.pallas import tpu as pltpu
from jax.sharding import PartitionSpec as P

SLICES = 4
CAP = 16
EPS = 1e-06
MESH = pl.DeviceIdType.MESH
F32 = jnp.float32
BF16 = jnp.bfloat16


def remote(src, dst, send, recv, device):
    return pltpu.make_async_remote_copy(
        src_ref=src,
        dst_ref=dst,
        send_sem=send,
        recv_sem=recv,
        device_id=device,
        device_id_type=MESH,
    )


def rows_contract(lhs, rhs):
    return lax.dot_general(lhs, rhs, (((0,), (0,)), ((), ())), preferred_element_type=F32)


def kernel(
    owners,
    tokens_ref,
    gain_ref,
    router_ref,
    wg_ref,
    wu_ref,
    wd_ref,
    picked_ref,
    out_ref,
    w_cat,
    w_down,
    ssq,
    normed,
    ranked,
    ranked_in,
    take,
    place_t,
    out_buf,
    in_buf,
    rows,
    acc,
    hidden,
    gate,
    core_out,
    core_in,
    own_part,
    y_out,
    y_in,
    x_out,
    x_in,
    ret_out,
    ret_in,
    w_sem,
    ssq_send,
    ssq_recv,
    disp_sem,
    ag_send,
    ag_recv,
    core_send,
    core_recv,
    y_send,
    y_recv,
    x_sem,
    ret_sem,
):
    tok_dev, quarter = tokens_ref.shape
    experts_n, capacity = picked_ref.shape
    sub = quarter // SLICES
    hid = wg_ref.shape[2]
    me = lax.axis_index("expert")
    y = lax.axis_index("mp")
    core = lax.rem(me, 2)
    pair = lax.rem(me // 2, 2)
    my_slice = lax.rem(me, SLICES)
    my_expert = me // SLICES
    sib = (me + 1 - 2 * core, y)
    xpart = (me + 2 - 4 * pair, y)
    y_up = lax.rem(y + 1, 4)
    y_down = lax.rem(y + 3, 4)
    y_far = lax.rem(y + 2, 4)
    up, down = (me, y_up), (me, y_down)

    def peer(r):
        return (lax.rem(me + r, owners), y)

    w_copies = [
        pltpu.make_async_copy(wg_ref.at[0], w_cat.at[:, pl.ds(0, hid)], w_sem.at[0]),
        pltpu.make_async_copy(wu_ref.at[0], w_cat.at[:, pl.ds(hid, hid)], w_sem.at[1]),
        pltpu.make_async_copy(wd_ref.at[0], w_down, w_sem.at[2]),
    ]
    for copy in w_copies:
        copy.start()

    barrier = pltpu.get_barrier_semaphore()

    def greet(r, carry):
        pl.semaphore_signal(barrier, inc=1, device_id=peer(r), device_id_type=MESH)
        return carry

    lax.fori_loop(1, owners, greet, 0)
    for r in range(1, 4):
        pl.semaphore_signal(
            barrier, inc=1, device_id=(me, lax.rem(y + r, 4)), device_id_type=MESH
        )

    lanes = 128
    part = jnp.zeros((tok_dev, lanes), F32)
    for j in range(quarter // lanes):
        piece = tokens_ref[:, j * lanes : (j + 1) * lanes].astype(F32)
        part = part + piece * piece
    ssq[0] = jnp.broadcast_to(jnp.sum(part.T, axis=0, keepdims=True), (8, tok_dev))

    pl.semaphore_wait(barrier, owners - 1 + 3)

    ssq_copies = [
        remote(
            ssq.at[0],
            ssq.at[r],
            ssq_send.at[r - 1],
            ssq_recv.at[r - 1],
            (me, lax.rem(y + r, 4)),
        )
        for r in range(1, 4)
    ]
    for copy in ssq_copies:
        copy.start()

    tri = (
        lax.broadcasted_iota(jnp.int32, (capacity, capacity), 0)
        <= lax.broadcasted_iota(jnp.int32, (capacity, capacity), 1)
    ).astype(F32).astype(BF16)
    rel = picked_ref[...] - me * tok_dev
    mine = (rel >= 0) & (rel < tok_dev)
    mine_f = jnp.where(mine, 1.0, 0.0)
    count = jnp.dot(mine_f.astype(BF16), tri, preferred_element_type=F32)
    ranked[0] = count * mine_f
    ranked[1] = rel.astype(F32)
    slot_no = lax.broadcasted_iota(jnp.int32, (CAP, capacity), 0).astype(F32) + 1.0
    lane_no = lax.broadcasted_iota(jnp.int32, (CAP, tok_dev), 1).astype(F32)
    for e in range(experts_n):
        hit = ranked[0, e : e + 1, :] == slot_no
        chosen = jnp.where(hit, ranked[1, e : e + 1, :] + 1.0, 0.0)
        token = jnp.sum(chosen, axis=1, keepdims=True) - 1.0
        take[e * CAP : (e + 1) * CAP, :] = jnp.where(token == lane_no, 1.0, 0.0).astype(BF16)

    row = picked_ref[pl.ds(my_expert, 1), :]
    low = lax.broadcasted_iota(jnp.int32, (owners, capacity), 0) * tok_dev
    held = jnp.where((row >= low) & (row < low + tok_dev), 1.0, 0.0)
    count_in = jnp.dot(held.astype(BF16), tri, preferred_element_type=F32)
    ranked_in[...] = count_in * held

    def place_owner(i, carry):
        at = pl.multiple_of(i * CAP, CAP)
        hit = ranked_in[pl.ds(i, 1), :] == slot_no
        place_t[pl.ds(at, CAP), :] = jnp.where(hit, 1.0, 0.0).astype(BF16)
        return carry

    lax.fori_loop(0, owners, place_owner, 0)

    for copy in ssq_copies:
        copy.wait_recv()
    total = ssq[0] + ssq[1] + ssq[2] + ssq[3]
    inv = lax.rsqrt(total * (1.0 / (4 * quarter)) + EPS)
    inv = jnp.broadcast_to(inv[0:1, :], (lanes, tok_dev)).T
    for j in range(quarter // lanes):
        cols = slice(j * lanes, (j + 1) * lanes)
        normed[:, cols] = (
            tokens_ref[:, cols].astype(F32) * inv * gain_ref[:, cols].astype(F32)
        ).astype(BF16)

    for s in range(SLICES):
        part_rows = jnp.dot(
            take[...], normed[:, s * sub : (s + 1) * sub], preferred_element_type=F32
        ).astype(BF16)
        for e in range(experts_n):
            out_buf[e * SLICES + s] = part_rows[e * CAP : (e + 1) * CAP, :]

    def dispatch(r, carry):
        d, _ = peer(r)
        remote(
            out_buf.at[d], in_buf.at[me], disp_sem.at[0], disp_sem.at[1], (d, y)
        ).start()
        return carry

    lax.fori_loop(1, owners, dispatch, 0)
    pltpu.make_async_copy(out_buf.at[me], in_buf.at[me], disp_sem.at[1]).start()

    select = jnp.where(
        lax.broadcasted_iota(jnp.int32, (experts_n, lanes), 0) == my_expert, 1.0, 0.0
    ).astype(BF16)
    for j in range(8):
        span = 4 * quarter // 8
        w_cat[j * span : (j + 1) * span, 2 * hid :] = jnp.dot(
            router_ref[j * span : (j + 1) * span, :], select, preferred_element_type=F32
        ).astype(BF16)
    w_copies[0].wait()
    w_copies[1].wait()

    pltpu.make_async_copy(in_buf, in_buf, disp_sem.at[1]).wait()

    def block(at_y, at_pair, at_core):
        return at_y * 4 + at_pair * 2 + at_core

    def ag(b, k, device):
        return remote(rows.at[b], rows.at[b], ag_send.at[k], ag_recv.at[b], device)

    def ag_arrived(b):
        ag(b, 0, sib).wait_recv()

    other = 1 - pair
    own = block(y, pair, core)
    rows[own] = rows_contract(
        place_t[...], in_buf[...].reshape(owners * CAP, sub)
    ).astype(BF16)

    def product(b):
        start = pl.multiple_of(b * sub, sub)
        return jnp.dot(
            rows[b], w_cat[pl.ds(start, sub), :], preferred_element_type=F32
        )

    sends = []

    def go(b, *devices):
        for device in devices:
            copy = ag(b, len(sends), device)
            copy.start()
            sends.append(copy)

    go(own, xpart, up, down, sib)
    acc[...] = product(own)

    def sibling_block(at_y, at_pair):
        b = block(at_y, at_pair, 1 - core)
        ag_arrived(b)
        acc[...] += product(b)

    def own_block(at_y, at_pair, *devices):
        b = block(at_y, at_pair, core)
        ag_arrived(b)
        go(b, *devices, sib)
        acc[...] += product(b)

    own_block(y, other, up, down)
    sibling_block(y, pair)
    own_block(y_down, pair, up)
    own_block(y_up, pair)
    sibling_block(y, other)
    own_block(y_up, other, down)
    own_block(y_down, other)
    sibling_block(y_down, pair)
    sibling_block(y_up, pair)
    sibling_block(y_up, other)
    sibling_block(y_down, other)
    own_block(y_far, pair)
    own_block(y_far, other)
    sibling_block(y_far, pair)
    sibling_block(y_far, other)

    hidden[...] = (
        jax.nn.gelu(acc[:, :hid], approximate=True) * acc[:, hid : 2 * hid]
    ).astype(BF16)
    gate[...] = jax.nn.sigmoid(acc[:, 2 * hid :]).astype(BF16).astype(F32)
    w_copies[2].wait()

    order = [
        (y_far, other),
        (y_far, pair),
        (y_up, other),
        (y_down, other),
        (y_up, pair),
        (y_down, pair),
        (y, other),
        (y, pair),
    ]

    def partial(at_y, at_pair, at_core):
        start = pl.multiple_of(block(at_y, at_pair, at_core) * sub, sub)
        return jnp.dot(
            hidden[...], w_down[:, pl.ds(start, sub)], preferred_element_type=F32
        )

    core_copies = []
    for k, (at_y, at_pair) in enumerate(order):
        core_out[k] = partial(at_y, at_pair, 1 - core).astype(BF16)
        copy = remote(core_out.at[k], core_in.at[k], core_send.at[k], core_recv.at[k], sib)
        copy.start()
        core_copies.append(copy)

    y_copies = []

    def y_go(k, value, device):
        y_out[k] = value.astype(BF16)
        copy = remote(y_out.at[k], y_in.at[k], y_send.at[k], y_recv.at[k], device)
        copy.start()
        y_copies.append(copy)

    def y_arrived(k):
        remote(y_out.at[k], y_in.at[k], y_send.at[k], y_recv.at[k], up).wait_recv()
        return y_in[k].astype(F32)

    def chip_sum(k):
        mine_now = partial(*order[k], core)
        core_copies[k].wait_recv()
        return mine_now + core_in[k].astype(F32)

    y_go(0, chip_sum(0), up)
    y_go(4, chip_sum(1), down)
    own_part[0] = chip_sum(2)
    y_go(3, chip_sum(3), down)
    y_go(2, chip_sum(4), up)
    own_part[1] = chip_sum(5)
    own_part[2] = chip_sum(6)
    own_part[3] = chip_sum(7)
    y_go(1, own_part[0] + y_arrived(0), up)
    y_go(5, own_part[1] + y_arrived(4), down)
    x_out[...] = (own_part[2] + y_arrived(1) + y_arrived(3)).astype(BF16)
    x_copy = remote(x_out, x_in, x_sem.at[0], x_sem.at[1], xpart)
    x_copy.start()
    total_out = own_part[3] + y_arrived(2) + y_arrived(5)
    x_copy.wait_recv()
    total_out = total_out + x_in[...].astype(F32)

    gate_wide = jnp.concatenate([gate[...]] * (sub // lanes), axis=1)
    gated = (total_out * gate_wide).astype(BF16)
    ret_out[...] = (
        jnp.dot(place_t[...], gated, preferred_element_type=F32)
        .astype(BF16)
        .reshape(owners, CAP, sub)
    )
    back = my_slice * experts_n + my_expert

    def give_back(r, carry):
        d, _ = peer(r)
        remote(
            ret_out.at[d], ret_in.at[back], ret_sem.at[0], ret_sem.at[1], (d, y)
        ).start()
        return carry

    lax.fori_loop(1, owners, give_back, 0)
    pltpu.make_async_copy(ret_out.at[me], ret_in.at[back], ret_sem.at[1]).start()

    for copy in ssq_copies + sends + core_copies + y_copies + [x_copy]:
        copy.wait_send()
    most = pl.ds(0, owners - 1)
    pltpu.make_async_copy(out_buf.at[most], out_buf.at[most], disp_sem.at[0]).wait()

    pltpu.make_async_copy(ret_in, ret_in, ret_sem.at[1]).wait()
    for s in range(SLICES):
        arrived = ret_in[s * experts_n : (s + 1) * experts_n].reshape(experts_n * CAP, sub)
        out_ref[:, s * sub : (s + 1) * sub] = rows_contract(take[...], arrived).astype(BF16)
    pltpu.make_async_copy(ret_out.at[most], ret_out.at[most], ret_sem.at[0]).wait()


def per_device(tokens, norm_gain, router, w_gate, w_up, w_down, picked):
    tok_dev, quarter = tokens.shape
    experts_n, capacity = picked.shape
    owners = lax.axis_size("expert")
    sub = quarter // SLICES
    hid = w_gate.shape[2]
    width = 4 * quarter
    dma = pltpu.SemaphoreType.DMA
    vmem = pl.BlockSpec(memory_space=pltpu.VMEM)
    hbm = pl.BlockSpec(memory_space=pl.ANY)
    return pl.pallas_call(
        functools.partial(kernel, owners),
        out_shape=jax.ShapeDtypeStruct((tok_dev, quarter), BF16),
        in_specs=[vmem, vmem, vmem, hbm, hbm, hbm, vmem],
        out_specs=vmem,
        scratch_shapes=[
            pltpu.VMEM((width, 2 * hid + 128), BF16),
            pltpu.VMEM((hid, width), BF16),
            pltpu.VMEM((4, 8, tok_dev), F32),
            pltpu.VMEM((tok_dev, quarter), BF16),
            pltpu.VMEM((2, experts_n, capacity), F32),
            pltpu.VMEM((owners, capacity), F32),
            pltpu.VMEM((experts_n * CAP, tok_dev), BF16),
            pltpu.VMEM((owners * CAP, capacity), BF16),
            pltpu.VMEM((owners, CAP, sub), BF16),
            pltpu.VMEM((owners, CAP, sub), BF16),
            pltpu.VMEM((16, capacity, sub), BF16),
            pltpu.VMEM((capacity, 2 * hid + 128), F32),
            pltpu.VMEM((capacity, hid), BF16),
            pltpu.VMEM((capacity, 128), F32),
            pltpu.VMEM((8, capacity, sub), BF16),
            pltpu.VMEM((8, capacity, sub), BF16),
            pltpu.VMEM((4, capacity, sub), F32),
            pltpu.VMEM((6, capacity, sub), BF16),
            pltpu.VMEM((6, capacity, sub), BF16),
            pltpu.VMEM((capacity, sub), BF16),
            pltpu.VMEM((capacity, sub), BF16),
            pltpu.VMEM((owners, CAP, sub), BF16),
            pltpu.VMEM((owners, CAP, sub), BF16),
            dma((3,)),
            dma((3,)),
            dma((3,)),
            dma((2,)),
            dma((15,)),
            dma((16,)),
            dma((8,)),
            dma((8,)),
            dma((6,)),
            dma((6,)),
            dma((2,)),
            dma((2,)),
        ],
        compiler_params=pltpu.CompilerParams(
            collective_id=0, has_side_effects=True, vmem_limit_bytes=56 * 1024 * 1024
        ),
        cost_estimate=pl.CostEstimate(
            flops=2 * capacity * width * 3 * hid,
            bytes_accessed=3 * 2 * width * hid + 4 * tok_dev * quarter,
            transcendentals=capacity * hid,
        ),
    )(tokens, norm_gain.reshape(1, quarter), router, w_gate, w_up, w_down, picked)


def solution(mesh):
    return jax.shard_map(
        per_device,
        mesh=mesh,
        in_specs=(
            P("expert", "mp"),
            P("mp"),
            P(),
            P("expert", None, "mp"),
            P("expert", None, "mp"),
            P("expert", "mp", None),
            P(),
        ),
        out_specs=P("expert", "mp"),
        check_vma=False,
    )
```

time: 662 us -> 111 us (0.17); the launches traced: 651 us -> 111 us
  waiting for transfers between devices: 265 us -> 0 us
  local copies, waits for them, and re-layouts: 226 us -> 5.75 us
  Pallas kernels: 0 us -> 105 us
  other arithmetic: 68.7 us -> 0 us
  starting transfers between devices: 37.9 us -> 0 us
  blocking collectives: 20.5 us -> 0 us
  matrix products: 19.2 us -> 0 us
  between operations: 13.8 us -> 0.01 us
    gather x8 -> x0, local copies, waits for them, and re-layouts: 174 us -> none  [the longest x2 153 us: per_device(): jnp.take_along_axis(running, owner_of[:, :, None], axis=2)[:, :, 0] - 1]
    all_to_all x3 -> x0, waiting for transfers between devices: 141 us -> none  [the longest x1 94.3 us: per_device(): lax.all_to_all(returning, 'expert', split_axis=0, concat_axis=0, tiled=True)]
    pallas_call x0 -> x1, Pallas kernels: none -> 105 us  [per_device(): pl.pallas_call(functools.partial(kernel, owners), out_shape=jax.ShapeDtyp...]
    reduce_scatter x1 -> x0, waiting for transfers between devices: 81.1 us -> none  [per_device(): lax.psum_scatter(jnp.transpose(product.reshape(capacity, lax.axis_size('m...]
    all_gather x1 -> x0, waiting for transfers between devices: 42.6 us -> none  [per_device(): shard_piece = lax.all_gather(picked_rows, 'mp', axis=1, tiled=True)]
    another operation x3 -> x0, other arithmetic: 39.4 us -> none
    all_to_all x3 -> x0, starting transfers between devices: 37.6 us -> none  [the longest x1 17.7 us: per_device(): lax.all_to_all(gate_out, 'expert', split_axis=0, concat_axis=0, tiled=True)]
    unnamed x16 -> x2, local copies, waits for them, and re-layouts: 30.5 us -> 4.48 us
  transfers between devices with their start and end apart: 5 -> 0, of which waited for: 5 -> 0; matrix products, arithmetic and copies ran while one was open for 3% -> 0% of each run, Pallas kernels for 0% -> 0%
where the time goes in v1:
time: 111 us
  Pallas kernels  105 us (95%)
  local copies, waits for them, and re-layouts  5.75 us (5%)
    pallas_call x1, Pallas kernels, per_device(): pl.pallas_call(functools.partial(kernel, owners), out_shape=jax.ShapeDtyp...  105 us
    unnamed x2, local copies, waits for them, and re-layouts  4.48 us

profile of v1, /device:TPU:1, one launch (start us, length us, event | category | flops | bytes accessed | tf_op | source)
XLA Modules:
  0.0 110.6 jit_solution(1171400440330104558)
XLA Ops:
  0.0 1.3 %reshape.3.gain_ref = bf16[1,1024]{1,0:T(2,128)(2,1)} reshape(bf16[1024]{0:T(1024)(128)(2,1)} %param.8) | data formatting | bytes 4096 | tf_op jit(solution)/shard_map/reshape | solution.py:428
  1.3 2.2 %copy.8.router_ref = bf16[4096,16]{1,0:T(8,128)(2,1)} copy(bf16[4096,16]{0,1:T(8,128)(2,1)} %param.9) | data formatting | bytes 262144 | tf_op args[2]
  3.5 104.8 %shard_map.73 = bf16[512,1024]{1,0:T(8,128)(2,1)} custom-call(bf16[512,1024]{1,0:T(8,128)(2,1)} %tokens_ref.1, bf16[1,1024]{1,0:T(2,128)(2,1)} %reshape.3.gain_ref, bf16[4096,16]{1,0:T(8,128)(2,1)} %copy.8.router_ref, bf16[1,4096,384]{2,1,0:T(8,128)(2,1)} %wg_ref.1, bf16[1,4096,384]{2,1,0:T(8,128)(2,1)} %wu_ref.1, bf16[1,384,4096]{2,1,0:T(8,128)(2,1)} %wd_ref.1, ...), custom_call_target="tpu_custom_call" | custom-call | flops 4831838208 | bytes 11534336 | tf_op jit(solution)/shard_map/pallas_call | solution.py:378
  108.3 2.3 %copy.10 = bf16[512,1024]{1,0:T(8,128)(2,1)} copy(bf16[512,1024]{1,0:T(8,128)(2,1)} %shard_map.73) | data formatting | bytes 2097152

commit v2 on v1

v2 whole, which is shorter than its diff:
```python
import functools

import jax
import jax.numpy as jnp
from jax import lax
from jax.experimental import pallas as pl
from jax.experimental.pallas import tpu as pltpu
from jax.sharding import PartitionSpec as P

SLICES = 4
CAP = 16
PARTS = 2
LANES = 128
EPS = 1e-06
MESH = pl.DeviceIdType.MESH
F32 = jnp.float32
BF16 = jnp.bfloat16


def remote(src, dst, send, recv, device):
    return pltpu.make_async_remote_copy(
        src_ref=src,
        dst_ref=dst,
        send_sem=send,
        recv_sem=recv,
        device_id=device,
        device_id_type=MESH,
    )


def dot(lhs, rhs):
    return jnp.dot(lhs, rhs, preferred_element_type=F32)


def one_hot(condition):
    return jnp.where(condition, 1.0, 0.0).astype(BF16)


def iota(shape, dim):
    return lax.broadcasted_iota(jnp.int32, shape, dim).astype(F32)


def kernel(
    owners,
    tokens_ref,
    gain_ref,
    router_ref,
    wg_ref,
    wu_ref,
    wd_ref,
    picked_ref,
    out_ref,
    w_cat,
    w_down,
    gains,
    gains_f,
    ranked,
    chosen_tok,
    take,
    take_t,
    place,
    place_t,
    out_buf,
    in_buf,
    rows,
    acc,
    squares,
    hidden,
    gate,
    core_out,
    core_in,
    keep,
    y_out,
    y_in,
    x_out,
    x_in,
    ret_out,
    ret_in,
    w_sem,
    gain_send,
    gain_recv,
    disp_send,
    disp_recv,
    ag_send,
    ag_recv,
    core_send,
    core_recv,
    y_send,
    y_recv,
    x_send,
    x_recv,
    ret_send,
    ret_recv,
):
    tok_dev, quarter = tokens_ref.shape
    experts_n, capacity = picked_ref.shape
    hid = wg_ref.shape[2]
    width = 4 * quarter
    half = capacity // 2
    both = 2 * LANES
    me = lax.axis_index("expert")
    y = lax.axis_index("mp")
    core = lax.rem(me, 2)
    pair = lax.rem(me // 2, 2)
    other = 1 - pair
    my_slice = lax.rem(me, SLICES)
    my_expert = me // SLICES
    sib = (me + 1 - 2 * core, y)
    xpart = (me + 2 - 4 * pair, y)
    y_up = lax.rem(y + 1, 4)
    y_down = lax.rem(y + 3, 4)
    y_far = lax.rem(y + 2, 4)
    up, down = (me, y_up), (me, y_down)

    def peer(r):
        return (lax.rem(me + r, owners), y)

    w_copies = [
        pltpu.make_async_copy(wg_ref.at[0], w_cat.at[:, pl.ds(0, hid)], w_sem.at[0]),
        pltpu.make_async_copy(wu_ref.at[0], w_cat.at[:, pl.ds(hid, hid)], w_sem.at[1]),
        pltpu.make_async_copy(wd_ref.at[0], w_down, w_sem.at[2]),
    ]
    for copy in w_copies:
        copy.start()

    barrier = pltpu.get_barrier_semaphore()

    def greet(r, carry):
        pl.semaphore_signal(barrier, inc=1, device_id=peer(r), device_id_type=MESH)
        return carry

    for r in range(1, 4):
        pl.semaphore_signal(
            barrier, inc=1, device_id=(me, lax.rem(y + r, 4)), device_id_type=MESH
        )
    lax.fori_loop(1, owners, greet, 0)

    tri = one_hot(iota((capacity, capacity), 0) <= iota((capacity, capacity), 1))
    rel = picked_ref[...] - me * tok_dev
    mine = jnp.where((rel >= 0) & (rel < tok_dev), 1.0, 0.0)
    ranked[0] = dot(mine.astype(BF16), tri) * mine
    ranked[1] = rel.astype(F32) + 1.0
    slot_no = iota((CAP, capacity), 0) + 1.0
    lane_no = iota((CAP, tok_dev), 1)
    for e in range(experts_n):
        hit = ranked[0, e : e + 1, :] == slot_no
        found = jnp.where(hit, ranked[1, e : e + 1, :], 0.0)
        token = jnp.sum(found, axis=1, keepdims=True) - 1.0
        take[e * CAP : (e + 1) * CAP, :] = one_hot(token == lane_no)
        chosen_tok[e * CAP : (e + 1) * CAP, :] = jnp.broadcast_to(token, (CAP, LANES))

    def gather(part):
        for p in range(2):
            start = p * quarter // 2 + part * both
            found = dot(take[...], tokens_ref[:, start : start + both]).astype(BF16)
            for e in range(experts_n):
                for c in range(2):
                    out_buf[part, e * SLICES + p * 2 + c] = found[
                        e * CAP : (e + 1) * CAP, c * LANES : (c + 1) * LANES
                    ]

    gather(0)
    gains[y] = jnp.concatenate([gain_ref[...], gain_ref[...]], axis=0)

    pl.semaphore_wait(barrier, owners - 1 + 3)

    def dispatch(part):
        def start(r, carry):
            d, _ = peer(r)
            remote(
                out_buf.at[part, d],
                in_buf.at[part, me],
                disp_send.at[part],
                disp_recv.at[part],
                (d, y),
            ).start()
            return carry

        lax.fori_loop(1, owners, start, 0)
        pltpu.make_async_copy(
            out_buf.at[part, me], in_buf.at[part, me], disp_recv.at[part]
        ).start()

    gain_copies = []
    for r in range(1, 4):
        copy = remote(
            gains.at[y],
            gains.at[y],
            gain_send.at[r - 1],
            gain_recv.at[y],
            (me, lax.rem(y + r, 4)),
        )
        copy.start()
        gain_copies.append(copy)
    dispatch(0)
    gather(1)
    dispatch(1)

    row = picked_ref[pl.ds(my_expert, 1), :]
    low = lax.broadcasted_iota(jnp.int32, (owners, capacity), 0) * tok_dev
    held = jnp.where((row >= low) & (row < low + tok_dev), 1.0, 0.0)
    slot_at = dot(held.astype(BF16), tri) - 1.0 + iota((owners, capacity), 0) * CAP
    flat = jnp.sum(held * slot_at, axis=0, keepdims=True)
    flat_col = jnp.broadcast_to(flat, (LANES, capacity)).T
    down_no = iota((LANES, capacity), 0)
    across_no = iota((capacity, LANES), 1)
    for j in range(owners * CAP // LANES):
        span = slice(j * LANES, (j + 1) * LANES)
        place_t[span, :] = one_hot(flat == down_no + j * LANES)
        place[:, span] = one_hot(flat_col == across_no + j * LANES)
    take_t[...] = one_hot(chosen_tok[...].T[0:1, :] == iota((tok_dev, experts_n * CAP), 0))

    select = one_hot(iota((experts_n, LANES), 0) == my_expert.astype(F32))
    for r in range(1, 4):
        at = lax.rem(y + r, 4)
        remote(gains.at[at], gains.at[at], gain_send.at[0], gain_recv.at[at], up).wait_recv()
    for at in range(4):
        gains_f[at * 8 : (at + 1) * 8, :] = gains[at][:8, :].astype(F32)
    w_copies[0].wait()
    w_copies[1].wait()

    def scale(q, carry):
        start = pl.multiple_of(q * LANES, LANES)
        column = jnp.broadcast_to(gains_f[pl.ds(q, 1), :], (LANES, LANES)).T
        for j in range(2 * hid // LANES):
            cols = slice(j * LANES, (j + 1) * LANES)
            w_cat[pl.ds(start, LANES), cols] = (
                w_cat[pl.ds(start, LANES), cols].astype(F32) * column
            ).astype(BF16)
        routed = lax.dot_general(
            router_ref[:, pl.ds(start, LANES)],
            select,
            (((0,), (0,)), ((), ())),
            preferred_element_type=F32,
        )
        w_cat[pl.ds(start, LANES), 2 * hid :] = (routed * column).astype(BF16)
        return carry

    lax.fori_loop(0, width // LANES, scale, 0)

    def block(at_y, at_pair):
        return at_y * 2 + at_pair

    def ag(part, b, c, h, k, device):
        at = rows.at[part, b, c, pl.ds(h * half, half)]
        number = ((part * 8 + b) * 2 + c) * 2 + h
        return remote(at, at, ag_send.at[k], ag_recv.at[number], device)

    sends = []

    def go(part, b, h, *devices):
        for device in devices:
            copy = ag(part, b, core, h, len(sends), device)
            copy.start()
            sends.append(copy)

    def pass_on(part, b, h, *devices):
        ag(part, b, core, h, 0, sib).wait_recv()
        go(part, b, h, *devices, sib)

    def begin(part):
        pltpu.make_async_copy(in_buf.at[part], in_buf.at[part], disp_recv.at[part]).wait()
        b = block(y, pair)
        rows[part, b, core] = dot(
            place[...], in_buf[part].reshape(owners * CAP, LANES)
        ).astype(BF16)
        for h in range(2):
            go(part, b, h, xpart, up, down, sib)

    def from_neighbours(part):
        pass_on(part, block(y_down, pair), 0, up)
        pass_on(part, block(y_up, pair), 1, down)
        pass_on(part, block(y_down, pair), 1)
        pass_on(part, block(y_up, pair), 0)

    def from_partner(part):
        for h in range(2):
            pass_on(part, block(y, other), h, up, down)

    def from_far(part):
        for h in range(2):
            pass_on(part, block(y_far, pair), h, xpart)

    def from_corners(part):
        for h in range(2):
            pass_on(part, block(y_down, other), h)
            pass_on(part, block(y_up, other), h)

    def from_far_corner(part):
        for h in range(2):
            pass_on(part, block(y_far, other), h)

    def product(part, at_y, at_pair, first=False):
        b = block(at_y, at_pair)
        for h in range(2):
            ag(part, b, 1 - core, h, 0, sib).wait_recv()
        start = pl.multiple_of(
            at_y * quarter + at_pair * (quarter // 2) + part * both, both
        )
        left, right = rows[part, b, 0], rows[part, b, 1]
        new = dot(jnp.concatenate([left, right], axis=1), w_cat[pl.ds(start, both), :])
        left, right = left.astype(F32), right.astype(F32)
        square = left * left + right * right
        if first:
            acc[...] = new
            squares[...] = square
        else:
            acc[...] += new
            squares[...] += square

    begin(0)
    from_neighbours(0)
    begin(1)
    from_partner(0)
    product(0, y, pair, first=True)
    product(0, y_down, pair)
    product(0, y_up, pair)
    product(0, y, other)
    from_far(0)
    from_neighbours(1)
    from_partner(1)
    from_corners(0)
    product(1, y, pair)
    product(0, y_far, pair)
    product(1, y_down, pair)
    product(1, y_up, pair)
    product(1, y, other)
    from_far(1)
    from_far_corner(0)
    product(0, y_down, other)
    product(0, y_up, other)
    product(0, y_far, other)
    from_corners(1)
    from_far_corner(1)
    product(1, y_far, pair)
    product(1, y_down, other)
    product(1, y_up, other)
    product(1, y_far, other)

    total = jnp.sum(squares[...], axis=1, keepdims=True)
    inv = lax.rsqrt(total * (1.0 / width) + EPS)
    hidden[...] = (
        jax.nn.gelu(acc[:, :hid] * inv, approximate=True) * (acc[:, hid : 2 * hid] * inv)
    ).astype(BF16)
    gate[...] = jax.nn.sigmoid(acc[:, 2 * hid :] * inv).astype(BF16).astype(F32)
    w_copies[2].wait()

    targets = [
        (y_far, other),
        (y_up, other),
        (y_down, other),
        (y_far, pair),
        (y_up, pair),
        (y_down, pair),
        (y, other),
        (y, pair),
    ]
    top, bottom = slice(0, half), slice(half, capacity)
    core_copies = {}

    def partials(part):
        for k, (at_y, at_pair) in enumerate(targets):
            start = pl.multiple_of(
                at_y * quarter + at_pair * (quarter // 2) + part * both, both
            )
            both_cores = dot(hidden[...], w_down[:, pl.ds(start, both)])
            low_half, high_half = both_cores[:, :LANES], both_cores[:, LANES:]
            keep[part, k] = jnp.where(core == 0, low_half, high_half)
            core_out[part, k] = jnp.where(core == 0, high_half, low_half).astype(BF16)
            number = part * 8 + k
            copy = remote(
                core_out.at[part, k],
                core_in.at[part, k],
                core_send.at[number],
                core_recv.at[number],
                sib,
            )
            copy.start()
            core_copies[part, k] = copy

    def chip(part, k):
        core_copies[part, k].wait_recv()
        return keep[part, k] + core_in[part, k].astype(F32)

    moved = []

    def y_copy(part, way, m):
        number = (part * 2 + way) * 5 + m
        return remote(
            y_out.at[part, way, m],
            y_in.at[part, way, m],
            y_send.at[number],
            y_recv.at[number],
            (up, down)[way],
        )

    def y_go(part, way, m, value):
        y_out[part, way, m] = value.astype(BF16)
        copy = y_copy(part, way, m)
        copy.start()
        moved.append(copy)

    def y_got(part, way, m):
        y_copy(part, way, m).wait_recv()
        return y_in[part, way, m].astype(F32)

    def x_copy(part, m):
        number = part * 4 + m
        return remote(
            x_out.at[part, m], x_in.at[part, m], x_send.at[number], x_recv.at[number], xpart
        )

    def x_go(part, m, value):
        x_out[part, m] = value.astype(BF16)
        copy = x_copy(part, m)
        copy.start()
        moved.append(copy)

    def x_got(part, m):
        x_copy(part, m).wait_recv()
        return x_in[part, m].astype(F32)

    def send_other(part):
        value = chip(part, 0)
        x_go(part, 0, value[top])
        x_go(part, 1, value[bottom])
        for way in range(2):
            value = chip(part, 1 + way)
            y_go(part, way, 0, value[top])
            y_go(part, way, 1, value[bottom])

    def send_direct(part):
        value = chip(part, 4)
        y_go(part, 0, 2, value[top])
        keep[part, 4, bottom] = value[bottom]
        value = chip(part, 5)
        y_go(part, 1, 2, value[bottom])
        keep[part, 5, top] = value[top]

    def send_far(part):
        value = chip(part, 3)
        y_go(part, 1, 3, value[top] + x_got(part, 0))
        y_go(part, 0, 3, value[bottom] + x_got(part, 1))

    def send_merged(part):
        y_go(part, 1, 4, keep[part, 5, top] + y_got(part, 1, 3))
        y_go(part, 0, 4, keep[part, 4, bottom] + y_got(part, 0, 3))

    def send_partner(part):
        value = chip(part, 6)
        x_go(part, 2, value[top] + y_got(part, 0, 0) + y_got(part, 1, 0))
        x_go(part, 3, value[bottom] + y_got(part, 0, 1) + y_got(part, 1, 1))

    back = my_slice * experts_n + my_expert

    def give_back(part):
        value = chip(part, 7)
        upper = value[top] + y_got(part, 0, 2) + y_got(part, 1, 4) + x_got(part, 2)
        lower = value[bottom] + y_got(part, 1, 2) + y_got(part, 0, 4) + x_got(part, 3)
        gated = (jnp.concatenate([upper, lower], axis=0) * gate[...]).astype(BF16)
        ret_out[part] = dot(place_t[...], gated).astype(BF16).reshape(owners, CAP, LANES)

        def start(r, carry):
            d, _ = peer(r)
            remote(
                ret_out.at[part, d],
                ret_in.at[part, back],
                ret_send.at[part],
                ret_recv.at[part],
                (d, y),
            ).start()
            return carry

        lax.fori_loop(1, owners, start, 0)
        pltpu.make_async_copy(
            ret_out.at[part, me], ret_in.at[part, back], ret_recv.at[part]
        ).start()

    partials(0)
    send_other(0)
    send_direct(0)
    partials(1)
    send_far(0)
    send_other(1)
    send_partner(0)
    send_merged(0)
    send_far(1)
    send_direct(1)
    send_partner(1)
    send_merged(1)
    give_back(0)
    give_back(1)

    most = pl.ds(0, owners - 1)
    for copy in gain_copies + sends + list(core_copies.values()) + moved:
        copy.wait_send()
    for part in range(PARTS):
        sent = out_buf.at[part, most]
        pltpu.make_async_copy(sent, sent, disp_send.at[part]).wait()

    for part in range(PARTS):
        pltpu.make_async_copy(ret_in.at[part], ret_in.at[part], ret_recv.at[part]).wait()
        for p in range(2):
            sides = [
                ret_in[part, (p * 2 + c) * experts_n : (p * 2 + c + 1) * experts_n].reshape(
                    experts_n * CAP, LANES
                )
                for c in range(2)
            ]
            start = p * quarter // 2 + part * both
            out_ref[:, start : start + both] = dot(
                take_t[...], jnp.concatenate(sides, axis=1)
            ).astype(BF16)
    for part in range(PARTS):
        sent = ret_out.at[part, most]
        pltpu.make_async_copy(sent, sent, ret_send.at[part]).wait()


def per_device(tokens, norm_gain, router, w_gate, w_up, w_down, picked):
    tok_dev, quarter = tokens.shape
    experts_n, capacity = picked.shape
    owners = lax.axis_size("expert")
    hid = w_gate.shape[2]
    width = 4 * quarter
    half = capacity // 2
    slots = experts_n * CAP
    dma = pltpu.SemaphoreType.DMA
    vmem = pl.BlockSpec(memory_space=pltpu.VMEM)
    hbm = pl.BlockSpec(memory_space=pl.ANY)
    return pl.pallas_call(
        functools.partial(kernel, owners),
        out_shape=jax.ShapeDtypeStruct((tok_dev, quarter), BF16),
        in_specs=[vmem, vmem, vmem, hbm, hbm, hbm, vmem],
        out_specs=vmem,
        scratch_shapes=[
            pltpu.VMEM((width, 2 * hid + LANES), BF16),
            pltpu.VMEM((hid, width), BF16),
            pltpu.VMEM((4, 16, LANES), BF16),
            pltpu.VMEM((32, LANES), F32),
            pltpu.VMEM((2, experts_n, capacity), F32),
            pltpu.VMEM((slots, LANES), F32),
            pltpu.VMEM((slots, tok_dev), BF16),
            pltpu.VMEM((tok_dev, slots), BF16),
            pltpu.VMEM((capacity, owners * CAP), BF16),
            pltpu.VMEM((owners * CAP, capacity), BF16),
            pltpu.VMEM((PARTS, owners, CAP, LANES), BF16),
            pltpu.VMEM((PARTS, owners, CAP, LANES), BF16),
            pltpu.VMEM((PARTS, 8, 2, capacity, LANES), BF16),
            pltpu.VMEM((capacity, 2 * hid + LANES), F32),
            pltpu.VMEM((capacity, LANES), F32),
            pltpu.VMEM((capacity, hid), BF16),
            pltpu.VMEM((capacity, LANES), F32),
            pltpu.VMEM((PARTS, 8, capacity, LANES), BF16),
            pltpu.VMEM((PARTS, 8, capacity, LANES), BF16),
            pltpu.VMEM((PARTS, 8, capacity, LANES), F32),
            pltpu.VMEM((PARTS, 2, 5, half, LANES), BF16),
            pltpu.VMEM((PARTS, 2, 5, half, LANES), BF16),
            pltpu.VMEM((PARTS, 4, half, LANES), BF16),
            pltpu.VMEM((PARTS, 4, half, LANES), BF16),
            pltpu.VMEM((PARTS, owners, CAP, LANES), BF16),
            pltpu.VMEM((PARTS, owners, CAP, LANES), BF16),
            dma((3,)),
            dma((3,)),
            dma((4,)),
            dma((PARTS,)),
            dma((PARTS,)),
            dma((60,)),
            dma((64,)),
            dma((16,)),
            dma((16,)),
            dma((20,)),
            dma((20,)),
            dma((8,)),
            dma((8,)),
            dma((PARTS,)),
            dma((PARTS,)),
        ],
        compiler_params=pltpu.CompilerParams(
            collective_id=0, has_side_effects=True, vmem_limit_bytes=56 * 1024 * 1024
        ),
        cost_estimate=pl.CostEstimate(
            flops=2 * capacity * width * 3 * hid,
            bytes_accessed=3 * 2 * width * hid + 4 * tok_dev * quarter,
            transcendentals=capacity * hid,
        ),
    )(
        tokens,
        norm_gain.reshape(quarter // LANES, LANES),
        router.T,
        w_gate,
        w_up,
        w_down,
        picked,
    )


def solution(mesh):
    return jax.shard_map(
        per_device,
        mesh=mesh,
        in_specs=(
            P("expert", "mp"),
            P("mp"),
            P(),
            P("expert", None, "mp"),
            P("expert", None, "mp"),
            P("expert", "mp", None),
            P(),
        ),
        out_specs=P("expert", "mp"),
        check_vma=False,
    )
```

time: 111 us -> 86.9 us (0.78)
  Pallas kernels: 105 us -> 84.5 us
  local copies, waits for them, and re-layouts: 5.75 us -> 2.26 us
    pallas_call x1, Pallas kernels: 105 us -> 84.5 us  [per_device(): pl.pallas_call(functools.partial(kernel, owners), out_shape=jax.ShapeDtyp...]
    unnamed x2 -> x1, local copies, waits for them, and re-layouts: 4.48 us -> 2.26 us
    reshape x1 -> x0, local copies, waits for them, and re-layouts: 1.27 us -> none  [per_device(): norm_gain.reshape(1, quarter)]
where the time goes in v2:
time: 86.9 us; the launch traced here: 86.7 us
  Pallas kernels  84.5 us (97%)
  local copies, waits for them, and re-layouts  2.26 us (3%)
    pallas_call x1, Pallas kernels, per_device(): pl.pallas_call(functools.partial(kernel, owners), out_shape=jax.ShapeDtyp...  84.5 us
    unnamed x1, local copies, waits for them, and re-layouts  2.26 us

profile of v2, /device:TPU:1, one launch (start us, length us, event | category | flops | bytes accessed | tf_op | source)
XLA Modules:
  0.0 86.7 jit_solution(15795689325307288193)
XLA Ops:
  0.0 84.5 %shard_map.73 = bf16[512,1024]{1,0:T(8,128)(2,1)} custom-call(bf16[512,1024]{1,0:T(8,128)(2,1)} %tokens_ref.1, bf16[8,128]{1,0:T(8,128)(2,1)} %bitcast.3, bf16[16,4096]{1,0:T(8,128)(2,1)} %bitcast.2, bf16[1,4096,384]{2,1,0:T(8,128)(2,1)} %wg_ref.1, bf16[1,4096,384]{2,1,0:T(8,128)(2,1)} %wu_ref.1, bf16[1,384,4096]{2,1,0:T(8,128)(2,1)} %wd_ref.1, ...), custom_call_target="tpu_custom_call" | custom-call | flops 4831838208 | bytes 11534336 | tf_op jit(solution)/shard_map/pallas_call | solution.py:530
  84.5 2.3 %copy.9 = bf16[512,1024]{1,0:T(8,128)(2,1)} copy(bf16[512,1024]{1,0:T(8,128)(2,1)} %shard_map.73) | data formatting | bytes 2097152

commit v3 on v2

--- a/solution.py
+++ b/solution.py
@@ -42,14 +42,18 @@
 
 def kernel(
     owners,
+    tokens_hbm,
+    gain_hbm,
+    router_hbm,
+    wg_ref,
+    wu_ref,
+    wd_ref,
+    picked_hbm,
+    out_ref,
     tokens_ref,
     gain_ref,
     router_ref,
-    wg_ref,
-    wu_ref,
-    wd_ref,
     picked_ref,
-    out_ref,
     w_cat,
     w_down,
     gains,
@@ -76,6 +80,7 @@
     x_in,
     ret_out,
     ret_in,
+    in_sem,
     w_sem,
     gain_send,
     gain_recv,
@@ -115,14 +120,6 @@
     def peer(r):
         return (lax.rem(me + r, owners), y)
 
-    w_copies = [
-        pltpu.make_async_copy(wg_ref.at[0], w_cat.at[:, pl.ds(0, hid)], w_sem.at[0]),
-        pltpu.make_async_copy(wu_ref.at[0], w_cat.at[:, pl.ds(hid, hid)], w_sem.at[1]),
-        pltpu.make_async_copy(wd_ref.at[0], w_down, w_sem.at[2]),
-    ]
-    for copy in w_copies:
-        copy.start()
-
     barrier = pltpu.get_barrier_semaphore()
 
     def greet(r, carry):
@@ -135,7 +132,26 @@
         )
     lax.fori_loop(1, owners, greet, 0)
 
+    in_copies = [
+        pltpu.make_async_copy(src, dst, in_sem.at[k])
+        for k, (src, dst) in enumerate(
+            [
+                (picked_hbm, picked_ref),
+                (tokens_hbm, tokens_ref),
+                (gain_hbm, gain_ref),
+                (router_hbm, router_ref),
+            ]
+        )
+    ]
+    w_copies = [
+        pltpu.make_async_copy(wg_ref.at[0], w_cat.at[:, pl.ds(0, hid)], w_sem.at[0]),
+        pltpu.make_async_copy(wu_ref.at[0], w_cat.at[:, pl.ds(hid, hid)], w_sem.at[1]),
+    ]
+    for copy in in_copies + w_copies:
+        copy.start()
+
     tri = one_hot(iota((capacity, capacity), 0) <= iota((capacity, capacity), 1))
+    in_copies[0].wait()
     rel = picked_ref[...] - me * tok_dev
     mine = jnp.where((rel >= 0) & (rel < tok_dev), 1.0, 0.0)
     ranked[0] = dot(mine.astype(BF16), tri) * mine
@@ -148,53 +164,6 @@
         token = jnp.sum(found, axis=1, keepdims=True) - 1.0
         take[e * CAP : (e + 1) * CAP, :] = one_hot(token == lane_no)
         chosen_tok[e * CAP : (e + 1) * CAP, :] = jnp.broadcast_to(token, (CAP, LANES))
-
-    def gather(part):
-        for p in range(2):
-            start = p * quarter // 2 + part * both
-            found = dot(take[...], tokens_ref[:, start : start + both]).astype(BF16)
-            for e in range(experts_n):
-                for c in range(2):
-                    out_buf[part, e * SLICES + p * 2 + c] = found[
-                        e * CAP : (e + 1) * CAP, c * LANES : (c + 1) * LANES
-                    ]
-
-    gather(0)
-    gains[y] = jnp.concatenate([gain_ref[...], gain_ref[...]], axis=0)
-
-    pl.semaphore_wait(barrier, owners - 1 + 3)
-
-    def dispatch(part):
-        def start(r, carry):
-            d, _ = peer(r)
-            remote(
-                out_buf.at[part, d],
-                in_buf.at[part, me],
-                disp_send.at[part],
-                disp_recv.at[part],
-                (d, y),
-            ).start()
-            return carry
-
-        lax.fori_loop(1, owners, start, 0)
-        pltpu.make_async_copy(
-            out_buf.at[part, me], in_buf.at[part, me], disp_recv.at[part]
-        ).start()
-
-    gain_copies = []
-    for r in range(1, 4):
-        copy = remote(
-            gains.at[y],
-            gains.at[y],
-            gain_send.at[r - 1],
-            gain_recv.at[y],
-            (me, lax.rem(y + r, 4)),
-        )
-        copy.start()
-        gain_copies.append(copy)
-    dispatch(0)
-    gather(1)
-    dispatch(1)
 
     row = picked_ref[pl.ds(my_expert, 1), :]
     low = lax.broadcasted_iota(jnp.int32, (owners, capacity), 0) * tok_dev
@@ -210,7 +179,91 @@
         place[:, span] = one_hot(flat_col == across_no + j * LANES)
     take_t[...] = one_hot(chosen_tok[...].T[0:1, :] == iota((tok_dev, experts_n * CAP), 0))
 
+    def gather(part):
+        for p in range(2):
+            start = p * quarter // 2 + part * both
+            found = dot(take[...], tokens_ref[:, start : start + both]).astype(BF16)
+            for e in range(experts_n):
+                for c in range(2):
+                    out_buf[part, e * SLICES + p * 2 + c] = found[
+                        e * CAP : (e + 1) * CAP, c * LANES : (c + 1) * LANES
+                    ]
+
+    in_copies[1].wait()
+    gather(0)
+    gather(1)
+    in_copies[2].wait()
+    in_copies[3].wait()
     select = one_hot(iota((experts_n, LANES), 0) == my_expert.astype(F32))
+    for j in range(8):
+        span = slice(j * width // 8, (j + 1) * width // 8)
+        w_cat[span, 2 * hid :] = lax.dot_general(
+            router_ref[:, span],
+            select,
+            (((0,), (0,)), ((), ())),
+            preferred_element_type=F32,
+        ).astype(BF16)
+    gains[y] = jnp.concatenate([gain_ref[...], gain_ref[...]], axis=0)
+
+    pl.semaphore_wait(barrier, owners - 1 + 3)
+
+    targets = [
+        (y_far, other),
+        (y_up, other),
+        (y_down, other),
+        (y_far, pair),
+        (y_up, pair),
+        (y_down, pair),
+        (y, other),
+        (y, pair),
+    ]
+
+    def load_down():
+        for part in range(PARTS):
+            for k, (at_y, at_pair) in enumerate(targets):
+                for side, c in enumerate((core, 1 - core)):
+                    start = at_y * quarter + at_pair * (quarter // 2) + part * both + c * LANES
+                    pltpu.make_async_copy(
+                        wd_ref.at[0, :, pl.ds(pl.multiple_of(start, LANES), LANES)],
+                        w_down.at[side, :, pl.ds((part * 8 + k) * LANES, LANES)],
+                        w_sem.at[2],
+                    ).start()
+
+    def dispatch(part):
+        for side in range(2):
+
+            def start(j, carry):
+                d = 2 * lax.rem(me // 2 + j, owners // 2) + side
+                remote(
+                    out_buf.at[part, d],
+                    in_buf.at[part, me],
+                    disp_send.at[part],
+                    disp_recv.at[part],
+                    (d, y),
+                ).start()
+                return carry
+
+            first = 1 - core if side == 0 else core
+            lax.fori_loop(first, owners // 2, start, 0)
+        pltpu.make_async_copy(
+            out_buf.at[part, me], in_buf.at[part, me], disp_recv.at[part]
+        ).start()
+
+    gain_copies = []
+    for r in range(1, 4):
+        copy = remote(
+            gains.at[y],
+            gains.at[y],
+            gain_send.at[r - 1],
+            gain_recv.at[y],
+            (me, lax.rem(y + r, 4)),
+        )
+        copy.start()
+        gain_copies.append(copy)
+    dispatch(0)
+    dispatch(1)
+    load_down()
+
     for r in range(1, 4):
         at = lax.rem(y + r, 4)
         remote(gains.at[at], gains.at[at], gain_send.at[0], gain_recv.at[at], up).wait_recv()
@@ -222,21 +275,14 @@
     def scale(q, carry):
         start = pl.multiple_of(q * LANES, LANES)
         column = jnp.broadcast_to(gains_f[pl.ds(q, 1), :], (LANES, LANES)).T
-        for j in range(2 * hid // LANES):
+        for j in range(2 * hid // LANES + 1):
             cols = slice(j * LANES, (j + 1) * LANES)
             w_cat[pl.ds(start, LANES), cols] = (
                 w_cat[pl.ds(start, LANES), cols].astype(F32) * column
             ).astype(BF16)
-        routed = lax.dot_general(
-            router_ref[:, pl.ds(start, LANES)],
-            select,
-            (((0,), (0,)), ((), ())),
-            preferred_element_type=F32,
-        )
-        w_cat[pl.ds(start, LANES), 2 * hid :] = (routed * column).astype(BF16)
         return carry
 
-    lax.fori_loop(0, width // LANES, scale, 0)
+    lax.fori_loop(0, width // LANES, scale, 0, unroll=4)
 
     def block(at_y, at_pair):
         return at_y * 2 + at_pair
@@ -265,17 +311,20 @@
             place[...], in_buf[part].reshape(owners * CAP, LANES)
         ).astype(BF16)
         for h in range(2):
-            go(part, b, h, xpart, up, down, sib)
+            go(part, b, h, xpart, up)
+            go(part, b, 1 - h, down)
+            go(part, b, h, sib)
 
     def from_neighbours(part):
         pass_on(part, block(y_down, pair), 0, up)
         pass_on(part, block(y_up, pair), 1, down)
+
+    def rest_of_neighbours(part):
         pass_on(part, block(y_down, pair), 1)
         pass_on(part, block(y_up, pair), 0)
 
-    def from_partner(part):
-        for h in range(2):
-            pass_on(part, block(y, other), h, up, down)
+    def from_partner(part, h):
+        pass_on(part, block(y, other), h, up, down)
 
     def from_far(part):
         for h in range(2):
@@ -310,31 +359,35 @@
 
     begin(0)
     from_neighbours(0)
+    from_partner(0, 0)
     begin(1)
-    from_partner(0)
+    from_partner(0, 1)
+    rest_of_neighbours(0)
     product(0, y, pair, first=True)
     product(0, y_down, pair)
+    from_far(0)
     product(0, y_up, pair)
+    from_neighbours(1)
+    from_partner(1, 0)
+    from_partner(1, 1)
+    rest_of_neighbours(1)
     product(0, y, other)
-    from_far(0)
-    from_neighbours(1)
-    from_partner(1)
-    from_corners(0)
     product(1, y, pair)
     product(0, y_far, pair)
+    from_corners(0)
     product(1, y_down, pair)
+    from_far(1)
     product(1, y_up, pair)
     product(1, y, other)
-    from_far(1)
     from_far_corner(0)
     product(0, y_down, other)
     product(0, y_up, other)
     product(0, y_far, other)
     from_corners(1)
-    from_far_corner(1)
     product(1, y_far, pair)
     product(1, y_down, other)
     product(1, y_up, other)
+    from_far_corner(1)
     product(1, y_far, other)
 
     total = jnp.sum(squares[...], axis=1, keepdims=True)
@@ -343,40 +396,37 @@
         jax.nn.gelu(acc[:, :hid] * inv, approximate=True) * (acc[:, hid : 2 * hid] * inv)
     ).astype(BF16)
     gate[...] = jax.nn.sigmoid(acc[:, 2 * hid :] * inv).astype(BF16).astype(F32)
-    w_copies[2].wait()
-
-    targets = [
-        (y_far, other),
-        (y_up, other),
-        (y_down, other),
-        (y_far, pair),
-        (y_up, pair),
-        (y_down, pair),
-        (y, other),
-        (y, pair),
-    ]
+    pltpu.make_async_copy(w_down, w_down, w_sem.at[2]).wait()
+
     top, bottom = slice(0, half), slice(half, capacity)
     core_copies = {}
 
-    def partials(part):
-        for k, (at_y, at_pair) in enumerate(targets):
-            start = pl.multiple_of(
-                at_y * quarter + at_pair * (quarter // 2) + part * both, both
-            )
-            both_cores = dot(hidden[...], w_down[:, pl.ds(start, both)])
-            low_half, high_half = both_cores[:, :LANES], both_cores[:, LANES:]
-            keep[part, k] = jnp.where(core == 0, low_half, high_half)
-            core_out[part, k] = jnp.where(core == 0, high_half, low_half).astype(BF16)
-            number = part * 8 + k
-            copy = remote(
-                core_out.at[part, k],
-                core_in.at[part, k],
-                core_send.at[number],
-                core_recv.at[number],
-                sib,
-            )
-            copy.start()
-            core_copies[part, k] = copy
+    def partial(part, k, side):
+        start = (part * 8 + k) * LANES
+        return dot(hidden[...], w_down[side, :, start : start + both])
+
+    def for_sibling(part, *firsts):
+        for first in firsts:
+            value = partial(part, first, 1)
+            for k in (first, first + 1):
+                at = (k - first) * LANES
+                core_out[part, k] = value[:, at : at + LANES].astype(BF16)
+                number = part * 8 + k
+                copy = remote(
+                    core_out.at[part, k],
+                    core_in.at[part, k],
+                    core_send.at[number],
+                    core_recv.at[number],
+                    sib,
+                )
+                copy.start()
+                core_copies[part, k] = copy
+
+    def for_me(part, *firsts):
+        for first in firsts:
+            value = partial(part, first, 0)
+            keep[part, first] = value[:, :LANES]
+            keep[part, first + 1] = value[:, LANES:]
 
     def chip(part, k):
         core_copies[part, k].wait_recv()
@@ -420,10 +470,12 @@
         x_copy(part, m).wait_recv()
         return x_in[part, m].astype(F32)
 
-    def send_other(part):
+    def send_corner(part):
         value = chip(part, 0)
         x_go(part, 0, value[top])
         x_go(part, 1, value[bottom])
+
+    def send_other(part):
         for way in range(2):
             value = chip(part, 1 + way)
             y_go(part, way, 0, value[top])
@@ -476,19 +528,29 @@
             ret_out.at[part, me], ret_in.at[part, back], ret_recv.at[part]
         ).start()
 
-    partials(0)
+    for_sibling(0, 0, 2)
+    for_me(0, 0)
+    send_corner(0)
+    for_me(0, 2)
     send_other(0)
+    for_sibling(0, 4)
+    for_me(0, 4)
     send_direct(0)
-    partials(1)
+    for_sibling(0, 6)
+    for_me(0, 6)
+    for_sibling(1, 0, 2, 4, 6)
     send_far(0)
+    for_me(1, 0, 2)
+    send_corner(1)
+    send_partner(0)
     send_other(1)
-    send_partner(0)
+    for_me(1, 4, 6)
     send_merged(0)
     send_far(1)
     send_direct(1)
     send_partner(1)
+    give_back(0)
     send_merged(1)
-    give_back(0)
     give_back(1)
 
     most = pl.ds(0, owners - 1)
@@ -530,11 +592,15 @@
     return pl.pallas_call(
         functools.partial(kernel, owners),
         out_shape=jax.ShapeDtypeStruct((tok_dev, quarter), BF16),
-        in_specs=[vmem, vmem, vmem, hbm, hbm, hbm, vmem],
+        in_specs=[hbm] * 7,
         out_specs=vmem,
         scratch_shapes=[
+            pltpu.VMEM((tok_dev, quarter), BF16),
+            pltpu.VMEM((quarter // LANES, LANES), BF16),
+            pltpu.VMEM((experts_n, width), BF16),
+            pltpu.VMEM((experts_n, capacity), jnp.int32),
             pltpu.VMEM((width, 2 * hid + LANES), BF16),
-            pltpu.VMEM((hid, width), BF16),
+            pltpu.VMEM((2, hid, width // 2), BF16),
             pltpu.VMEM((4, 16, LANES), BF16),
             pltpu.VMEM((32, LANES), F32),
             pltpu.VMEM((2, experts_n, capacity), F32),
@@ -559,6 +625,7 @@
             pltpu.VMEM((PARTS, 4, half, LANES), BF16),
             pltpu.VMEM((PARTS, owners, CAP, LANES), BF16),
             pltpu.VMEM((PARTS, owners, CAP, LANES), BF16),
+            dma((4,)),
             dma((3,)),
             dma((3,)),
             dma((4,)),

time: 86.9 us -> 78.9 us (0.908)
  Pallas kernels: 84.5 us -> 76.5 us
    pallas_call x1, Pallas kernels: 84.5 us -> 76.5 us  [per_device(): pl.pallas_call(functools.partial(kernel, owners), out_shape=jax.ShapeDtyp...]
where the time goes in v3:
time: 78.9 us; the launch traced here: 78.7 us
  Pallas kernels  76.5 us (97%)
  local copies, waits for them, and re-layouts  2.26 us (3%)
    pallas_call x1, Pallas kernels, per_device(): pl.pallas_call(functools.partial(kernel, owners), out_shape=jax.ShapeDtyp...  76.5 us
    unnamed x1, local copies, waits for them, and re-layouts  2.26 us

profile of v3, /device:TPU:1, one launch (start us, length us, event | category | flops | bytes accessed | tf_op | source)
XLA Modules:
  0.0 78.7 jit_solution(14173910256330556396)
XLA Ops:
  0.0 76.5 %shard_map.73 = bf16[512,1024]{1,0:T(8,128)(2,1)} custom-call(bf16[512,1024]{1,0:T(8,128)(2,1)} %tokens_hbm.1, bf16[8,128]{1,0:T(8,128)(2,1)} %bitcast.3, bf16[16,4096]{1,0:T(8,128)(2,1)} %bitcast.2, bf16[1,4096,384]{2,1,0:T(8,128)(2,1)} %wg_ref.1, bf16[1,4096,384]{2,1,0:T(8,128)(2,1)} %wu_ref.1, bf16[1,384,4096]{2,1,0:T(8,128)(2,1)} %wd_ref.1, ...), custom_call_target="tpu_custom_call" | custom-call | flops 4831838208 | bytes 11534336 | tf_op jit(solution)/shard_map/pallas_call | solution.py:592
  76.5 2.3 %copy.9 = bf16[512,1024]{1,0:T(8,128)(2,1)} copy(bf16[512,1024]{1,0:T(8,128)(2,1)} %shard_map.73) | data formatting | bytes 2097152

commit v4 on v3

--- a/solution.py
+++ b/solution.py
@@ -49,7 +49,8 @@
     wu_ref,
     wd_ref,
     picked_hbm,
-    out_ref,
+    ret_in,
+    take_hbm,
     tokens_ref,
     gain_ref,
     router_ref,
@@ -79,8 +80,8 @@
     x_out,
     x_in,
     ret_out,
-    ret_in,
     in_sem,
+    take_sem,
     w_sem,
     gain_send,
     gain_recv,
@@ -178,6 +179,8 @@
         place_t[span, :] = one_hot(flat == down_no + j * LANES)
         place[:, span] = one_hot(flat_col == across_no + j * LANES)
     take_t[...] = one_hot(chosen_tok[...].T[0:1, :] == iota((tok_dev, experts_n * CAP), 0))
+    take_copy = pltpu.make_async_copy(take_t, take_hbm, take_sem.at[0])
+    take_copy.start()
 
     def gather(part):
         for p in range(2):
@@ -560,22 +563,46 @@
         sent = out_buf.at[part, most]
         pltpu.make_async_copy(sent, sent, disp_send.at[part]).wait()
 
+    take_copy.wait()
     for part in range(PARTS):
+        sent = ret_out.at[part, most]
         pltpu.make_async_copy(ret_in.at[part], ret_in.at[part], ret_recv.at[part]).wait()
+        pltpu.make_async_copy(sent, sent, ret_send.at[part]).wait()
+
+
+def add_up(ret_hbm, take_hbm, out_hbm, ret, take_t, out, in_sem, out_sem):
+    slots = take_t.shape[1]
+    experts_n = slots // CAP
+    both = 2 * LANES
+    take_copy = pltpu.make_async_copy(take_hbm, take_t, in_sem.at[PARTS])
+    copies = [
+        pltpu.make_async_copy(ret_hbm.at[part], ret.at[part], in_sem.at[part])
+        for part in range(PARTS)
+    ]
+    take_copy.start()
+    for copy in copies:
+        copy.start()
+    take_copy.wait()
+    out_copies = []
+    for part in range(PARTS):
+        copies[part].wait()
         for p in range(2):
             sides = [
-                ret_in[part, (p * 2 + c) * experts_n : (p * 2 + c + 1) * experts_n].reshape(
-                    experts_n * CAP, LANES
+                ret[part, (p * 2 + c) * experts_n : (p * 2 + c + 1) * experts_n].reshape(
+                    slots, LANES
                 )
                 for c in range(2)
             ]
-            start = p * quarter // 2 + part * both
-            out_ref[:, start : start + both] = dot(
-                take_t[...], jnp.concatenate(sides, axis=1)
-            ).astype(BF16)
-    for part in range(PARTS):
-        sent = ret_out.at[part, most]
-        pltpu.make_async_copy(sent, sent, ret_send.at[part]).wait()
+            k = part * 2 + p
+            out[k] = dot(take_t[...], jnp.concatenate(sides, axis=1)).astype(BF16)
+            start = p * (PARTS * both) + part * both
+            copy = pltpu.make_async_copy(
+                out.at[k], out_hbm.at[:, pl.ds(start, both)], out_sem.at[k]
+            )
+            copy.start()
+            out_copies.append(copy)
+    for copy in out_copies:
+        copy.wait()
 
 
 def per_device(tokens, norm_gain, router, w_gate, w_up, w_down, picked):
@@ -587,13 +614,15 @@
     half = capacity // 2
     slots = experts_n * CAP
     dma = pltpu.SemaphoreType.DMA
-    vmem = pl.BlockSpec(memory_space=pltpu.VMEM)
     hbm = pl.BlockSpec(memory_space=pl.ANY)
-    return pl.pallas_call(
+    returned, take_t = pl.pallas_call(
         functools.partial(kernel, owners),
-        out_shape=jax.ShapeDtypeStruct((tok_dev, quarter), BF16),
+        out_shape=(
+            jax.ShapeDtypeStruct((PARTS, owners, CAP, LANES), BF16),
+            jax.ShapeDtypeStruct((tok_dev, slots), BF16),
+        ),
         in_specs=[hbm] * 7,
-        out_specs=vmem,
+        out_specs=(hbm, hbm),
         scratch_shapes=[
             pltpu.VMEM((tok_dev, quarter), BF16),
             pltpu.VMEM((quarter // LANES, LANES), BF16),
@@ -624,8 +653,8 @@
             pltpu.VMEM((PARTS, 4, half, LANES), BF16),
             pltpu.VMEM((PARTS, 4, half, LANES), BF16),
             pltpu.VMEM((PARTS, owners, CAP, LANES), BF16),
-            pltpu.VMEM((PARTS, owners, CAP, LANES), BF16),
             dma((4,)),
+            dma((1,)),
             dma((3,)),
             dma((3,)),
             dma((4,)),
@@ -659,6 +688,25 @@
         w_down,
         picked,
     )
+    return pl.pallas_call(
+        add_up,
+        out_shape=jax.ShapeDtypeStruct((tok_dev, quarter), BF16),
+        in_specs=[hbm, hbm],
+        out_specs=hbm,
+        scratch_shapes=[
+            pltpu.VMEM((PARTS, owners, CAP, LANES), BF16),
+            pltpu.VMEM((tok_dev, slots), BF16),
+            pltpu.VMEM((2 * PARTS, tok_dev, 2 * LANES), BF16),
+            dma((PARTS + 1,)),
+            dma((2 * PARTS,)),
+        ],
+        compiler_params=pltpu.CompilerParams(vmem_limit_bytes=56 * 1024 * 1024),
+        cost_estimate=pl.CostEstimate(
+            flops=2 * tok_dev * slots * quarter,
+            bytes_accessed=2 * (2 * slots + tok_dev) * quarter,
+            transcendentals=0,
+        ),
+    )(returned, take_t)
 
 
 def solution(mesh):

time: 78.9 us -> 78.3 us (level)
  local copies, waits for them, and re-layouts: 2.26 us -> 0 us
  Pallas kernels: 76.5 us -> 78.2 us
    unnamed x1 -> x0, local copies, waits for them, and re-layouts: 2.26 us -> none
    pallas_call x1 -> x2, Pallas kernels: 76.5 us -> 78.2 us  [the longest x1 75.7 us: per_device(): pl.pallas_call(functools.partial(kernel, owners), out_shape=(jax.ShapeDty...]
where the time goes in v4:
time: 78.3 us; the launch traced here: 78.2 us
  Pallas kernels  78.2 us (100%)
    pallas_call x1, Pallas kernels, per_device(): pl.pallas_call(functools.partial(kernel, owners), out_shape=(jax.ShapeDty...  75.7 us
    pallas_call x1, Pallas kernels, per_device(): pl.pallas_call(add_up, out_shape=jax.ShapeDtypeStruct((tok_dev, quarter),...  2.5 us

profile of v4, /device:TPU:1, one launch (start us, length us, event | category | flops | bytes accessed | tf_op | source)
XLA Modules:
  0.0 78.2 jit_solution(9234508733246380099)
XLA Ops:
  0.0 75.7 %shard_map.73 = (bf16[2,64,16,128]{3,2,1,0:T(8,128)(2,1)}, bf16[512,256]{1,0:T(8,128)(2,1)}) custom-call(bf16[512,1024]{1,0:T(8,128)(2,1)} %tokens_hbm.1, bf16[8,128]{1,0:T(8,128)(2,1)} %bitcast.3, bf16[16,4096]{1,0:T(8,128)(2,1)} %bitcast.2, bf16[1,4096,384]{2,1,0:T(8,128)(2,1)} %wg_ref.1, bf16[1,4096,384]{2,1,0:T(8,128)(2,1)} %wu_ref.1, ...), custom_call_target="tpu_custom_call" | custom-call | flops 4831838208 | bytes 11534336 | tf_op jit(solution)/shard_map/pallas_call | solution.py:618
  75.7 2.5 %shard_map.74 = bf16[512,1024]{1,0:T(8,128)(2,1)} custom-call(bf16[2,64,16,128]{3,2,1,0:T(8,128)(2,1)} %get-tuple-element.7.ret_hbm, bf16[512,256]{1,0:T(8,128)(2,1)} %get-tuple-element.8.take_hbm), custom_call_target="tpu_custom_call" | custom-call | flops 268435456 | bytes 2097152 | tf_op jit(solution)/shard_map/pallas_call | solution.py:691

commit v5 on v4

--- a/solution.py
+++ b/solution.py
@@ -364,22 +364,22 @@
     from_neighbours(0)
     from_partner(0, 0)
     begin(1)
+    from_neighbours(1)
     from_partner(0, 1)
+    from_partner(1, 0)
     rest_of_neighbours(0)
+    from_far(0)
+    from_partner(1, 1)
     product(0, y, pair, first=True)
     product(0, y_down, pair)
-    from_far(0)
     product(0, y_up, pair)
-    from_neighbours(1)
-    from_partner(1, 0)
-    from_partner(1, 1)
     rest_of_neighbours(1)
+    from_far(1)
     product(0, y, other)
     product(1, y, pair)
     product(0, y_far, pair)
     from_corners(0)
     product(1, y_down, pair)
-    from_far(1)
     product(1, y_up, pair)
     product(1, y, other)
     from_far_corner(0)

time: 78.3 us -> 77.4 us (0.989)
  Pallas kernels: 78.2 us -> 77.3 us
    pallas_call x1, Pallas kernels: 75.7 us -> 74.8 us  [per_device(): pl.pallas_call(functools.partial(kernel, owners), out_shape=(jax.ShapeDty...]
where the time goes in v5:
time: 77.4 us; the launch traced here: 77.3 us
  Pallas kernels  77.3 us (100%)
    pallas_call x1, Pallas kernels, per_device(): pl.pallas_call(functools.partial(kernel, owners), out_shape=(jax.ShapeDty...  74.8 us
    pallas_call x1, Pallas kernels, per_device(): pl.pallas_call(add_up, out_shape=jax.ShapeDtypeStruct((tok_dev, quarter),...  2.49 us

profile of v5, /device:TPU:1, one launch (start us, length us, event | category | flops | bytes accessed | tf_op | source)
XLA Modules:
  0.0 77.3 jit_solution(4467195135301615915)
XLA Ops:
  0.0 74.8 %shard_map.73 = (bf16[2,64,16,128]{3,2,1,0:T(8,128)(2,1)}, bf16[512,256]{1,0:T(8,128)(2,1)}) custom-call(bf16[512,1024]{1,0:T(8,128)(2,1)} %tokens_hbm.1, bf16[8,128]{1,0:T(8,128)(2,1)} %bitcast.3, bf16[16,4096]{1,0:T(8,128)(2,1)} %bitcast.2, bf16[1,4096,384]{2,1,0:T(8,128)(2,1)} %wg_ref.1, bf16[1,4096,384]{2,1,0:T(8,128)(2,1)} %wu_ref.1, ...), custom_call_target="tpu_custom_call" | custom-call | flops 4831838208 | bytes 11534336 | tf_op jit(solution)/shard_map/pallas_call | solution.py:618
  74.8 2.5 %shard_map.74 = bf16[512,1024]{1,0:T(8,128)(2,1)} custom-call(bf16[2,64,16,128]{3,2,1,0:T(8,128)(2,1)} %get-tuple-element.7.ret_hbm, bf16[512,256]{1,0:T(8,128)(2,1)} %get-tuple-element.8.take_hbm), custom_call_target="tpu_custom_call" | custom-call | flops 268435456 | bytes 2097152 | tf_op jit(solution)/shard_map/pallas_call | solution.py:691

commit v6 on v5

--- a/solution.py
+++ b/solution.py
@@ -310,13 +310,14 @@
     def begin(part):
         pltpu.make_async_copy(in_buf.at[part], in_buf.at[part], disp_recv.at[part]).wait()
         b = block(y, pair)
-        rows[part, b, core] = dot(
-            place[...], in_buf[part].reshape(owners * CAP, LANES)
-        ).astype(BF16)
+        arrived = in_buf[part].reshape(owners * CAP, LANES)
         for h in range(2):
-            go(part, b, h, xpart, up)
-            go(part, b, 1 - h, down)
-            go(part, b, h, sib)
+            span = slice(h * half, (h + 1) * half)
+            rows[part, b, core, span] = dot(place[span, :], arrived).astype(BF16)
+            if h == 1:
+                go(part, b, 1, down)
+            go(part, b, h, xpart, up, sib)
+        go(part, b, 0, down)
 
     def from_neighbours(part):
         pass_on(part, block(y_down, pair), 0, up)

time: 77.4 us -> 77.3 us (level)
  no operation moved by 1% of the time
where the time goes in v6:
time: 77.3 us; the launch traced here: 77.2 us
  Pallas kernels  77.2 us (100%)
    pallas_call x1, Pallas kernels, per_device(): pl.pallas_call(functools.partial(kernel, owners), out_shape=(jax.ShapeDty...  74.7 us
    pallas_call x1, Pallas kernels, per_device(): pl.pallas_call(add_up, out_shape=jax.ShapeDtypeStruct((tok_dev, quarter),...  2.49 us

profile of v6, /device:TPU:1, one launch (start us, length us, event | category | flops | bytes accessed | tf_op | source)
XLA Modules:
  0.0 77.2 jit_solution(13355478390249225676)
XLA Ops:
  0.0 74.7 %shard_map.73 = (bf16[2,64,16,128]{3,2,1,0:T(8,128)(2,1)}, bf16[512,256]{1,0:T(8,128)(2,1)}) custom-call(bf16[512,1024]{1,0:T(8,128)(2,1)} %tokens_hbm.1, bf16[8,128]{1,0:T(8,128)(2,1)} %bitcast.3, bf16[16,4096]{1,0:T(8,128)(2,1)} %bitcast.2, bf16[1,4096,384]{2,1,0:T(8,128)(2,1)} %wg_ref.1, bf16[1,4096,384]{2,1,0:T(8,128)(2,1)} %wu_ref.1, ...), custom_call_target="tpu_custom_call" | custom-call | flops 4831838208 | bytes 11534336 | tf_op jit(solution)/shard_map/pallas_call | solution.py:619
  74.7 2.5 %shard_map.74 = bf16[512,1024]{1,0:T(8,128)(2,1)} custom-call(bf16[2,64,16,128]{3,2,1,0:T(8,128)(2,1)} %get-tuple-element.7.ret_hbm, bf16[512,256]{1,0:T(8,128)(2,1)} %get-tuple-element.8.take_hbm), custom_call_target="tpu_custom_call" | custom-call | flops 268435456 | bytes 2097152 | tf_op jit(solution)/shard_map/pallas_call | solution.py:692
